TPU v7x, 32 devices: a whole 2x2x4 slice. The times are simulated.
32 devices in a mesh: wide: 8 (over y, x, core), narrow: 4 (over z).
Axes of the slice: x: 2, y: 2, z: 4, core: 2. Of those that a mesh axis runs over, the one named last changes fastest.
Arguments:
- tokens: bfloat16 [2048, 2048], P('wide', 'narrow'), may hold values from -6 to 6
- norm_gain: bfloat16 [2048], replicated, may hold values from 0.25 to 1.75
- router: bfloat16 [2048, 8], replicated, may hold values from -0.125 to 0.125
- routes: int32 [2048, 2], P('wide'), may hold values from 0 to 7, all different within a row
- kv_weight: bfloat16 [4096, 2048], P('narrow', 'wide'), may hold values from -0.125 to 0.125
- query_weight: bfloat16 [16384, 2048], P('narrow', 'wide'), may hold values from -0.125 to 0.125
- out_weight: bfloat16 [16384, 2048], P('narrow', 'wide'), may hold values from -0.09375 to 0.09375
- prefix_cache: bfloat16 [6144, 4096], P('wide', 'narrow'), may hold values from -225 to 225
- suffix_lengths: int32 [4], replicated, may hold values from 1 to 1280, 2048 in all
- prefix_lengths: int32 [4], replicated, may hold values from 1 to 3072, 6144 in all
Outputs:
- mixed: bfloat16 [2048, 2048], P('wide', 'narrow')
Inputs may be any that keep to these rules, and one draw needn't show every extreme that they name: `routes`: each token names 2 different experts. `suffix_lengths`: they sum to 2048. `prefix_lengths`: they sum to 6144.
All inputs are finite; a program needn't handle non-finite values.
Results may differ from a plain program's by a relative error of at most 0.012.
The roundings to bfloat16 on the way count: a program that leaves them out, or rounds other values in their place, can miss the bound.
Values may be sent and summed in bfloat16 or wider, within the bound.
A program may use at most 320 MiB of HBM per device.

v0:
```python
import math

import jax
import jax.numpy as jnp
from jax import lax
from jax.sharding import PartitionSpec as P

H = 128
E = 8


eps = 1e-06
floor_value = -1e30


def tenant_of(positions, lengths):
    bounds = jnp.cumsum(lengths)
    return jnp.sum((positions[:, None] >= bounds[None, :]).astype(jnp.int32), axis=1)


def attend(carried, queries, key_block, value_block, allowed, scaling):
    highest, totals, summed = carried
    scores = (
        jnp.einsum("hrd,nhd->hrn", queries, key_block, preferred_element_type=jnp.float32) * scaling
    )
    scores = jnp.where(allowed[None, :, :], scores, -jnp.inf)
    new_highest = jnp.maximum(highest, jnp.max(scores, axis=2))
    weights = jnp.exp(scores - new_highest[:, :, None])
    factor = jnp.exp(highest - new_highest)
    totals = totals * factor + jnp.sum(weights, axis=2)
    summed = summed * factor[:, :, None] + jnp.einsum(
        "hrn,nhd->hrd",
        weights,
        value_block.astype(jnp.float32),
        precision=lax.Precision.HIGHEST,
        preferred_element_type=jnp.float32,
    )
    return (new_highest, totals, summed)


def over_blocks(
    carried, queries, cache_rows, row_tenant, row_index, key_tenant, key_index, scaling, causal
):
    length = cache_rows.shape[0]
    block_size = math.gcd(length, 512)
    steps_count = length // block_size
    cache_blocks = cache_rows.reshape((steps_count, block_size) + cache_rows.shape[1:])
    tenant_blocks = key_tenant.reshape(steps_count, block_size)
    index_blocks = key_index.reshape(steps_count, block_size)

    def advance(current, inputs):
        rows_here, tenant_here, index_here = inputs
        allowed = row_tenant[:, None] == tenant_here[None, :]
        if causal:
            allowed = allowed & (index_here[None, :] <= row_index[:, None])
        return (
            attend(
                current, queries, rows_here[:, :, 0, :], rows_here[:, :, 1, :], allowed, scaling
            ),
            None,
        )

    carried, unused = lax.scan(advance, carried, (cache_blocks, tenant_blocks, index_blocks))
    return carried


def on_device(
    tokens,
    norm_gain,
    router,
    routes,
    kv_weight,
    query_weight,
    out_weight,
    prefix_cache,
    suffix_lengths,
    prefix_lengths,
):
    whole = lax.all_gather(tokens, "narrow", axis=1, tiled=True)
    tok_rows = whole.shape[0]
    local_heads = kv_weight.shape[0] // (2 * H)
    slot_count = routes.shape[1]
    scaling = H ** (-0.5)
    floats = whole.astype(jnp.float32)
    normed = (
        floats
        * lax.rsqrt(jnp.mean(floats * floats, axis=1, keepdims=True) + eps)
        * norm_gain.astype(jnp.float32)
    ).astype(jnp.bfloat16)
    logits = jnp.dot(normed, router, preferred_element_type=jnp.float32)
    one_hot = routes[:, :, None] == jnp.arange(E, dtype=jnp.int32)[None, None, :]
    chosen = jnp.sum(jnp.where(one_hot, logits[:, None, :], 0.0), axis=2)
    gate_values = jax.nn.softmax(chosen, axis=1)
    choose = one_hot.astype(jnp.bfloat16)
    kv_part = lax.dot_general(
        normed,
        lax.all_gather(kv_weight, "wide", axis=1, tiled=True),
        (((1,), (1,)), ((), ())),
        preferred_element_type=jnp.float32,
    )
    query_part = lax.dot_general(
        normed,
        lax.all_gather(query_weight, "wide", axis=1, tiled=True),
        (((1,), (1,)), ((), ())),
        preferred_element_type=jnp.float32,
    )
    kv_local = kv_part.astype(jnp.bfloat16).reshape(tok_rows, local_heads, 2, H)
    query_all = query_part.astype(jnp.bfloat16).reshape(tok_rows, local_heads, E, H)
    selected = jnp.einsum(
        "tje,thed->htjd", choose, query_all, preferred_element_type=jnp.float32
    ).astype(jnp.bfloat16)
    row_count = tok_rows * slot_count
    queries = selected.reshape(local_heads, row_count, H)
    first_token = lax.axis_index("wide") * tok_rows
    token_index = first_token + jnp.arange(tok_rows, dtype=jnp.int32)
    row_index = jnp.repeat(token_index, slot_count)
    row_tenant = tenant_of(row_index, suffix_lengths)
    start_carry = (
        jnp.full((local_heads, row_count), floor_value, jnp.float32),
        jnp.zeros((local_heads, row_count), jnp.float32),
        jnp.zeros((local_heads, row_count, H), jnp.float32),
    )
    shard_piece = lax.all_gather(prefix_cache, "wide", axis=0, tiled=True)
    piece_rows = shard_piece.shape[0]
    slot_index = jnp.arange(piece_rows, dtype=jnp.int32)
    slot_tenant = tenant_of(slot_index, prefix_lengths)
    cache_rows = shard_piece.reshape(piece_rows, local_heads, 2, H)
    carried = over_blocks(
        start_carry,
        queries,
        cache_rows,
        row_tenant,
        row_index,
        slot_tenant,
        slot_index,
        scaling,
        False,
    )
    shard_piece = lax.all_gather(kv_local, "wide", axis=0, tiled=True)
    piece_rows = shard_piece.shape[0]
    key_index = jnp.arange(piece_rows, dtype=jnp.int32)
    key_tenant = tenant_of(key_index, suffix_lengths)
    carried = over_blocks(
        carried, queries, shard_piece, row_tenant, row_index, key_tenant, key_index, scaling, True
    )
    highest, totals, summed = carried
    attended = (summed / totals[:, :, None]).reshape(local_heads, tok_rows, slot_count, H)
    weighted = (attended * gate_values[None, :, :, None]).astype(jnp.bfloat16)
    padded = (
        jnp.einsum("tje,htjd->thed", choose, weighted, preferred_element_type=jnp.float32)
        .astype(jnp.bfloat16)
        .reshape(tok_rows, local_heads * E * H)
    )
    partial_out = jnp.dot(
        padded,
        lax.all_gather(out_weight, "wide", axis=1, tiled=True),
        preferred_element_type=jnp.float32,
    )
    return lax.psum_scatter(partial_out, "narrow", scatter_dimension=1, tiled=True).astype(
        jnp.bfloat16
    )


def solution(mesh):
    placed = (
        P("wide", "narrow"),
        P(),
        P(),
        P("wide", None),
        P("narrow", "wide"),
        P("narrow", "wide"),
        P("narrow", "wide"),
        P("wide", "narrow"),
        P(),
        P(),
    )
    return jax.shard_map(
        on_device, mesh=mesh, in_specs=placed, out_specs=P("wide", "narrow"), check_vma=False
    )
```

profile of v0, /device:TPU:3, one launch (start us, length us, event | category | flops | bytes accessed | tf_op | source)
XLA Modules:
  0.0 514.1 jit_solution(17325089890246621767)
XLA Ops:
  9.4 28.6 %all-gather.9.cloned.1.call-done = bf16[256,2048]{1,0:T(8,128)(2,1)} async-done(((bf16[256,512]{1,0:T(8,128)(2,1)}), bf16[256,2048]{1,0:T(8,128)(2,1)}) %all-gather.9.cloned.1.call-update) | async-done | bytes 1048592 | tf_op jit(solution)/shard_map/all_gather | solution.py:79
  39.5 37.9 %all-gather.13.cloned.1.call-done = bf16[1024,2048]{1,0:T(8,128)(2,1)} async-done(((bf16[1024,256]{1,0:T(8,128)(2,1)}), bf16[1024,2048]{1,0:T(8,128)(2,1)}) %all-gather.13.cloned.1.call-update) | async-done | bytes 4194320 | tf_op jit(solution)/shard_map/all_gather | solution.py:97
  77.4 3.8 convolution_convert_fusion.2
  86.9 64.6 %all-gather.7.cloned.1.call-done = bf16[6144,1024]{1,0:T(8,128)(2,1)} async-done(((bf16[768,1024]{1,0:T(8,128)(2,1)}), bf16[6144,1024]{1,0:T(8,128)(2,1)}) %all-gather.7.cloned.1.call-update) | async-done | bytes 12582928 | tf_op jit(solution)/shard_map/all_gather | solution.py:123
  151.4 21.1 %reshape_reshape.3 = bf16[12,512,4,2,128]{4,3,2,1,0:T(2,128)(2,1)} reshape(bf16[6144,1024]{1,0:T(8,128)(2,1)} %all-gather.7.cloned.1.call-done) | data formatting | bytes 25165824 | tf_op jit(solution)/shard_map/reshape;reshape | solution.py:47
  172.6 73.7 %all-gather.11.cloned.1.call-done = bf16[4096,2048]{1,0:T(8,128)(2,1)} async-done(((bf16[4096,256]{1,0:T(8,128)(2,1)}), bf16[4096,2048]{1,0:T(8,128)(2,1)}) %all-gather.11.cloned.1.call-update) | async-done | bytes 16777232 | tf_op jit(solution)/shard_map/all_gather | solution.py:103
  246.3 8.5 %fusion.31 = bf16[32,8,32,128]{3,1,2,0:T(8,128)(2,1)S(1)} fusion(bf16[4096,2048]{1,0:T(8,128)(2,1)} %all-gather.11.cloned.1.call-done, bf16[256,2048]{1,0:T(8,128)(2,1)S(1)} %copy-done.4, f32[2048]{0:T(1024)S(1)} %convert_element_type.48, f32[256]{0:T(256)S(1)} %add_rsqrt_fusion), kind=kOutput, calls=%fused_computation.57 | convolution fusion | flops 4298113024 | bytes 19932160 | tf_op jit(solution)/shard_map/dot_general | solution.py:101
  256.8 158.5 %while.31 = (s32[]{:T(128)}, f32[4,512]{1,0:T(4,128)S(1)}, f32[4,512]{1,0:T(4,128)S(1)}, f32[4,512,128]{2,1,0:T(8,128)S(1)}, s32[512]{0:T(512)S(1)}, /*index=5*/...) while((s32[]{:T(128)}, f32[4,512]{1,0:T(4,128)S(1)}, ...), condition=%wide.region_8.9_spmd.clone, body=%wide.region_5.8_spmd.clone.sunk | while | flops 1890592768 | bytes 38412436 | solution.py:63
  259.3 2.8 fusion.67
  262.1 3.2 fusion.68
  265.5 4.5 fusion.70
  272.4 2.8 fusion.67
  275.1 3.3 fusion.68
  278.7 4.5 fusion.70
  285.5 2.8 fusion.67
  288.3 3.2 fusion.68
  291.7 4.5 fusion.70
  298.6 2.8 fusion.67
  301.4 3.3 fusion.68
  304.9 4.5 fusion.70
  311.7 2.8 fusion.67
  314.5 3.2 fusion.68
  317.9 4.5 fusion.70
  324.7 2.9 fusion.67
  327.7 4.3 fusion.68
  332.4 4.5 fusion.70
  339.3 2.8 fusion.67
  342.1 3.2 fusion.68
  345.5 4.5 fusion.70
  355.2 3.2 fusion.68
  358.6 4.5 fusion.70
  365.4 2.8 fusion.67
  368.2 3.2 fusion.68
  371.6 4.5 fusion.70
  381.2 3.2 fusion.68
  384.7 4.5 fusion.70
  391.5 2.8 fusion.67
  394.3 3.2 fusion.68
  397.7 4.5 fusion.70
  407.3 3.2 fusion.68
  410.8 4.5 fusion.70
  415.3 32.7 %while.30 = (s32[]{:T(128)}, f32[4,512]{1,0:T(4,128)S(1)}, f32[4,512]{1,0:T(4,128)S(1)}, f32[4,512,128]{2,1,0:T(8,128)S(1)}, s32[512]{0:T(512)S(1)}, /*index=5*/...) while((s32[]{:T(128)}, f32[4,512]{1,0:T(4,128)S(1)}, ...), condition=%wide.region_13.14_spmd.clone, body=%wide.region_10.13_spmd.clone.sunk | while | flops 1890848768 | bytes 19553904 | solution.py:63
  419.2 4.4 fusion.65
  427.3 4.4 fusion.65
  435.4 4.4 fusion.65
  443.5 4.4 fusion.65
  450.6 11.0 %fusion.28 = f32[256,2048]{1,0:T(8,128)} fusion(bf16[4096,2048]{1,0:T(8,128)(2,1)} %all-gather.17.cloned.1.call-done, bf16[32,8,32,128]{3,2,1,0:T(8,128)(2,1)S(1)} %bitcast.127), kind=kOutput, calls=%fused_computation.53 | convolution fusion | flops 4294967296 | bytes 20971520 | tf_op jit(solution)/shard_map/dot_general | solution.py:154
  461.6 43.9 %reduce-scatter.2.cloned.1.call-done = f32[256,512]{1,0:T(8,128)} async-done(((f32[256,2048]{1,0:T(8,128)}), f32[256,512]{1,0:T(8,128)}) %reduce-scatter.2.cloned.1.call-update) | async-done | bytes 524304 | tf_op jit(solution)/shard_map/reduce_scatter | solution.py:159
  (222 shorter events, 69.3 us)
Async XLA Ops:
  6.5 77.8 %copy-start = (bf16[2048,8]{0,1:T(8,128)(2,1)S(1)}, bf16[2048,8]{0,1:T(8,128)(2,1)}, u32[]{:S(2)}) copy-start(bf16[2048,8]{0,1:T(8,128)(2,1)} %param.16) | copy-start | bytes 98308
  6.5 2.8 copy-start.9
  6.5 31.4 %all-gather.9.cloned.1.call-start = ((), (), s32[]{:S(2)}) async-start(), calls=%async_computation.2 | async-start | bytes 1310720 | tf_op jit(solution)/shard_map/all_gather | solution.py:79
  7.3 70.1 %all-gather.13.cloned.1.call-start = ((), (), s32[]{:S(2)}) async-start(), calls=%async_computation.4 | async-start | bytes 4718592 | tf_op jit(solution)/shard_map/all_gather | solution.py:97
  8.0 143.4 %all-gather.7.cloned.1.call-start = ((), (), s32[]{:S(2)}) async-start(), calls=%async_computation.1 | async-start | bytes 14155776 | tf_op jit(solution)/shard_map/all_gather | solution.py:123
  8.7 237.6 %all-gather.11.cloned.1.call-start = ((), (), s32[]{:S(2)}) async-start(), calls=%async_computation.3 | async-start | bytes 18874368 | tf_op jit(solution)/shard_map/all_gather | solution.py:103
  9.3 406.0 %all-gather.15.cloned.1.call-start = ((), (), s32[]{:S(2)}) async-start(), calls=%async_computation.5 | async-start | bytes 4718592 | tf_op jit(solution)/shard_map/all_gather | solution.py:139
  81.2 2.0 copy-start.10
  81.2 2.2 copy-start.11
  81.2 2.8 copy-start.12
  81.2 3.1 copy-start.3
  82.5 368.0 %all-gather.17.cloned.1.call-start = ((), (), s32[]{:S(2)}) async-start(), calls=%async_computation.6 | async-start | bytes 18874368 | tf_op jit(solution)/shard_map/all_gather | solution.py:156
  83.1 422.3 %reduce-scatter.2.cloned.1.call-start = ((), (), s32[]{:S(2)}) async-start(), calls=%async_computation.7 | async-start | bytes 2621440 | tf_op jit(solution)/shard_map/reduce_scatter | solution.py:159
  83.4 172.0 %copy-start.6 = (s32[256,2]{1,0:T(8,128)}, s32[256,2]{1,0:T(8,128)S(1)}, u32[]{:S(2)}) copy-start(s32[256,2]{1,0:T(8,128)S(1)} %copy.27) | copy-start | bytes 6148
  86.9 159.5 %copy-start.4 = (bf16[256,2048]{1,0:T(8,128)(2,1)S(1)}, bf16[256,2048]{1,0:T(8,128)(2,1)}, u32[]{:S(2)}) copy-start(bf16[256,2048]{1,0:T(8,128)(2,1)} %all-gather.9.cloned.1.call-done) | copy-start | bytes 3145732
  255.3 1.4 copy-start.5
  262.1 3.4 copy-start.2
  275.1 3.5 copy-start.2
  288.3 3.4 copy-start.2
  301.4 3.5 copy-start.2
  314.5 3.4 copy-start.2
  327.7 4.8 copy-start.2
  342.1 3.4 copy-start.2
  355.1 3.4 copy-start.2
  368.2 3.4 copy-start.2
  381.2 3.4 copy-start.2
  394.3 3.4 copy-start.2
  407.3 3.4 copy-start.2
  415.3 33.0 %copy-start.7 = (s32[256,2]{1,0:T(8,128)S(1)}, s32[256,2]{1,0:T(8,128)}, u32[]{:S(2)}) copy-start(s32[256,2]{1,0:T(8,128)} %copy-done.6) | copy-start | bytes 6148
  415.3 33.0 %copy-start.8 = (f32[256,2]{1,0:T(8,128)S(1)}, f32[256,2]{1,0:T(8,128)}, u32[]{:S(2)}) copy-start(f32[256,2]{1,0:T(8,128)} %fusion.40) | copy-start | bytes 6148
  450.5 56.7 %copy-start.1 = (bf16[2048,8]{0,1:T(8,128)(2,1)S(1)}, bf16[2048,8]{0,1:T(8,128)(2,1)}, u32[]{:S(2)}) copy-start(bf16[2048,8]{0,1:T(8,128)(2,1)} %param.16) | copy-start | bytes 98308
Sparse Core Ops, SparseCore 0:
  8.9 29.0 all-gather.8
  39.9 37.4 all-gather.12
  79.3 72.1 all-gather.6
  153.2 93.1 all-gather.10
  248.1 36.7 all-gather.14
  286.6 93.1 all-gather.16
  461.7 43.7 reduce-scatter.1
where the time goes:
time: 517 us; the launch traced here: 514 us
  waiting for transfers between devices  252 us (49%)
  matrix products  135 us (26%)
  local copies, waits for them, and re-layouts  57.6 us (11%)
  other arithmetic  54.1 us (10%)
  between operations  13.8 us (3%)
    all_gather x1, waiting for transfers between devices, on_device(): lax.all_gather(query_weight, 'wide', axis=1, tiled=True)  73.7 us
    dot_general x16, matrix products, attend(): jnp.einsum('hrn,nhd->hrd', weights, value_block.astype(jnp.float32), prec...  71.2 us
    all_gather x1, waiting for transfers between devices, on_device(): shard_piece = lax.all_gather(prefix_cache, 'wide', axis=0, tiled=True)  64.6 us
    reduce_scatter x1, waiting for transfers between devices, on_device(): lax.psum_scatter(partial_out, 'narrow', scatter_dimension=1, tiled=True)  43.9 us
    reduce_sum x16, other arithmetic, attend(): totals = totals * factor + jnp.sum(weights, axis=2)  43.7 us
    all_gather x1, waiting for transfers between devices, on_device(): lax.all_gather(kv_weight, 'wide', axis=1, tiled=True)  37.9 us
    dot_general x16, matrix products, attend(): jnp.einsum('hrd,nhd->hrn', queries, key_block, preferred_element_type=jnp...  36.7 us
    all_gather x1, waiting for transfers between devices, on_device(): whole = lax.all_gather(tokens, 'narrow', axis=1, tiled=True)  28.6 us
  transfers between devices with their start and end apart: 7, of which 5 were waited for; matrix products, arithmetic and copies ran while one was open for 45% of the time, Pallas kernels for 0%

commit v1 on v0

v1 whole, which is shorter than its diff:
```python
import functools
import math

import jax
import jax.numpy as jnp
from jax import lax
from jax.experimental import pallas as pl
from jax.experimental.pallas import tpu as pltpu
from jax.sharding import PartitionSpec as P

H = 128
E = 8
EPS = 1e-06
FLOOR = -1e30
F32 = jnp.float32
BF16 = jnp.bfloat16
NT = (((1,), (1,)), ((), ()))
TN = (((0,), (0,)), ((), ()))


def pick(routes_column, blocks):
    found = jnp.zeros_like(blocks[0])
    for expert, block in enumerate(blocks):
        found = jnp.where(routes_column == expert, block, found)
    return found


def attend_kernel(
    group, suffix_ref, prefix_ref, sub_ref, normed_ref, router_ref, query_ref, routes_ref,
    cache_ref, kv_ref, out_ref
):
    block = normed_ref.shape[0]
    tenants = suffix_ref.shape[0]
    cache_rows = cache_ref.shape[0]
    cache_block = math.gcd(cache_rows, 512)
    strands = kv_ref.shape[0] // (group * block)
    token_block = pl.program_id(0) * group + sub_ref[0]
    first = token_block * block
    last = first + block - 1

    normed = normed_ref[...]
    logits = jnp.dot(normed, router_ref[...], preferred_element_type=F32)
    expert_at = lax.broadcasted_iota(jnp.int32, logits.shape, 1)
    route_a, route_b = routes_ref[:, 0:1], routes_ref[:, 1:2]
    logit_a = jnp.sum(jnp.where(expert_at == route_a, logits, 0.0), axis=1, keepdims=True)
    logit_b = jnp.sum(jnp.where(expert_at == route_b, logits, 0.0), axis=1, keepdims=True)
    top = jnp.maximum(logit_a, logit_b)
    up_a, up_b = jnp.exp(logit_a - top), jnp.exp(logit_b - top)
    gate_a, gate_b = up_a / (up_a + up_b), up_b / (up_a + up_b)

    every = lax.dot_general(normed, query_ref[...], NT, preferred_element_type=F32)
    parts = [every[:, e * H:(e + 1) * H] for e in range(E)]
    queries = jnp.concatenate([pick(route_a, parts), pick(route_b, parts)], axis=0).astype(BF16)

    token = first + lax.broadcasted_iota(jnp.int32, (1, block), 1)
    low = jnp.zeros((1, block), jnp.int32)
    high = jnp.zeros((1, block), jnp.int32)
    start = jnp.zeros((1, block), jnp.int32)
    low_block = jnp.int32(0)
    high_block = jnp.int32(0)
    start_block = jnp.int32(0)
    suffix_at = jnp.int32(0)
    prefix_at = jnp.int32(0)
    for tenant in range(tenants):
        suffix_end = suffix_at + suffix_ref[tenant]
        prefix_end = prefix_at + prefix_ref[tenant]
        inside = (token >= suffix_at) & (token < suffix_end)
        low = jnp.where(inside, prefix_at, low)
        high = jnp.where(inside, prefix_end, high)
        start = jnp.where(inside, suffix_at, start)
        holds_first = (first >= suffix_at) & (first < suffix_end)
        holds_last = (last >= suffix_at) & (last < suffix_end)
        low_block = jnp.where(holds_first, prefix_at, low_block)
        start_block = jnp.where(holds_first, suffix_at, start_block)
        high_block = jnp.where(holds_last, prefix_end, high_block)
        suffix_at, prefix_at = suffix_end, prefix_end
    twice = lambda row: jnp.concatenate([row, row], axis=1)
    low, high, start, upto = twice(low), twice(high), twice(start), twice(token + 1)
    to_log2 = math.log2(math.e) * H ** (-0.5)
    rows = 2 * block

    def over(carried, keys, values, key_first, row_low, row_high):
        highest, totals, summed = carried
        scores = lax.dot_general(keys, queries, NT, preferred_element_type=F32)
        at = key_first + lax.broadcasted_iota(jnp.int32, scores.shape, 0)
        scores = jnp.where((at >= row_low) & (at < row_high), scores, -jnp.inf)
        new_highest = jnp.maximum(highest, jnp.max(scores, axis=0, keepdims=True))
        weights = jnp.exp2((scores - new_highest) * to_log2)
        factor = jnp.exp2((highest - new_highest) * to_log2)
        totals = totals * factor + jnp.sum(weights, axis=0, keepdims=True)
        summed = summed * factor + lax.dot_general(
            values, weights.astype(BF16), TN, preferred_element_type=F32
        )
        return new_highest, totals, summed

    def over_cache(step, carried):
        at = pl.multiple_of(step * cache_block, cache_block)
        here = cache_ref[pl.ds(at, cache_block), :]
        return over(carried, here[:, :H], here[:, H:], at, low, high)

    def over_suffix(step, carried):
        place = lax.rem(step, group) * strands + lax.div(step, group)
        here = kv_ref[pl.ds(pl.multiple_of(place * block, block), block), :]
        return over(carried, here[:, :H], here[:, H:], step * block, start, upto)

    carried = (
        jnp.full((1, rows), FLOOR, F32),
        jnp.zeros((1, rows), F32),
        jnp.zeros((H, rows), F32),
    )
    carried = lax.fori_loop(
        lax.div(low_block, cache_block),
        lax.div(high_block + cache_block - 1, cache_block),
        over_cache,
        carried,
    )
    carried = lax.fori_loop(lax.div(start_block, block), token_block + 1, over_suffix, carried)
    unused, totals, summed = carried
    attended = jnp.transpose(summed / totals)
    out_ref[0] = (attended[:block] * gate_a).astype(BF16)
    out_ref[1] = (attended[block:] * gate_b).astype(BF16)


def out_kernel(attended_ref, weight_ref, routes_ref, out_ref):
    heads = attended_ref.shape[0]
    route_a, route_b = routes_ref[:, 0:1], routes_ref[:, 1:2]
    total = jnp.zeros(out_ref.shape, F32)
    for head in range(heads):
        first, second = attended_ref[head, 0, 0], attended_ref[head, 0, 1]
        nothing = jnp.zeros_like(first)
        padded = jnp.concatenate(
            [
                jnp.where(route_a == e, first, jnp.where(route_b == e, second, nothing))
                for e in range(E)
            ],
            axis=1,
        )
        total = total + jnp.dot(
            padded, weight_ref[head * E * H:(head + 1) * E * H, :], preferred_element_type=F32
        )
    out_ref[...] = total


def on_device(
    wide,
    narrow,
    tokens,
    norm_gain,
    router,
    routes,
    kv_weight,
    query_weight,
    out_weight,
    prefix_cache,
    suffix_lengths,
    prefix_lengths,
):
    block = tokens.shape[0]
    width = router.shape[0]
    heads = kv_weight.shape[0] // (2 * H)
    group = wide // heads
    strands = wide // group
    columns = width // wide
    me = lax.axis_index("wide")
    sub = lax.rem(me, group)
    same_sub = [[s + group * a for a in range(strands)] for s in range(group)]
    same_head = [[a * group + s for s in range(group)] for a in range(strands)]

    whole = lax.all_gather(tokens, "narrow", axis=1, tiled=True)
    floats = whole.astype(F32)
    normed = (
        floats
        * lax.rsqrt(jnp.mean(floats * floats, axis=1, keepdims=True) + EPS)
        * norm_gain.astype(F32)
    ).astype(BF16)
    normed = lax.all_gather(normed, "wide", axis_index_groups=same_sub, axis=0, tiled=True)
    routes_all = lax.all_gather(routes, "wide", axis=0, tiled=True)
    routes_here = lax.dynamic_slice_in_dim(
        routes_all.reshape(strands, group, block, 2), sub, 1, axis=1
    ).reshape(strands * block, 2)

    def spread(weight):
        mine = lax.all_to_all(weight, "wide", split_axis=0, concat_axis=1, tiled=True)
        return lax.all_gather(mine, "wide", axis_index_groups=same_head, axis=0, tiled=True)

    kv_rows = spread(kv_weight)
    query_rows = spread(query_weight)
    cache = lax.all_to_all(prefix_cache, "wide", split_axis=1, concat_axis=0, tiled=True)
    cache = lax.all_gather(cache, "wide", axis_index_groups=same_head, axis=1, tiled=True)

    kv = lax.dot_general(normed, kv_rows, NT, preferred_element_type=F32).astype(BF16)
    kv = lax.all_gather(kv, "wide", axis_index_groups=same_head, axis=0, tiled=True)

    whole_block = lambda array: pl.BlockSpec(array.shape, lambda i: (0,) * array.ndim)
    smem = pl.BlockSpec(memory_space=pltpu.SMEM)
    attended = pl.pallas_call(
        functools.partial(attend_kernel, group),
        grid=(strands,),
        out_shape=jax.ShapeDtypeStruct((2, strands * block, H), BF16),
        in_specs=[
            smem,
            smem,
            smem,
            pl.BlockSpec((block, width), lambda i: (i, 0)),
            whole_block(router),
            whole_block(query_rows),
            pl.BlockSpec((block, 2), lambda i: (i, 0)),
            whole_block(cache),
            whole_block(kv),
        ],
        out_specs=pl.BlockSpec((2, block, H), lambda i: (0, i, 0)),
        compiler_params=pltpu.CompilerParams(vmem_limit_bytes=56 * 1024 * 1024),
        name="attend",
    )(
        suffix_lengths, prefix_lengths, sub[None], normed, router, query_rows, routes_here, cache, kv
    )
    attended = lax.all_gather(attended, "wide", axis=0).reshape(
        heads, group, 2, strands * block, H
    )
    partial_out = pl.pallas_call(
        out_kernel,
        grid=(wide,),
        out_shape=jax.ShapeDtypeStruct((wide * block, columns), F32),
        in_specs=[
            pl.BlockSpec(
                (heads, 1, 2, block, H), lambda i: (0, lax.rem(i, group), 0, lax.div(i, group), 0)
            ),
            whole_block(out_weight),
            pl.BlockSpec((block, 2), lambda i: (i, 0)),
        ],
        out_specs=pl.BlockSpec((block, columns), lambda i: (i, 0)),
        compiler_params=pltpu.CompilerParams(vmem_limit_bytes=56 * 1024 * 1024),
        name="project_out",
    )(attended, out_weight, routes_all)
    mine = lax.psum_scatter(partial_out, "narrow", scatter_dimension=0, tiled=True).astype(BF16)
    ratio = wide // narrow
    mine = mine.reshape(ratio, block, columns)
    which = lax.rem(me, ratio)
    pieces = []
    for turn in range(ratio):
        chosen = lax.dynamic_index_in_dim(mine, lax.rem(which + turn, ratio), 0, keepdims=False)
        pairs = []
        for w in range(wide):
            for n in range(narrow):
                to_wide = ratio * n + (w % ratio + turn) % ratio
                to_narrow = w // ratio
                pairs.append((w * narrow + n, to_wide * narrow + to_narrow))
        pieces.append(lax.ppermute(chosen, ("wide", "narrow"), pairs))
    stacked = jnp.stack(pieces)
    ordered = [
        lax.dynamic_index_in_dim(stacked, lax.rem(which - k + ratio, ratio), 0, keepdims=False)
        for k in range(ratio)
    ]
    return jnp.concatenate(ordered, axis=1)


def solution(mesh):
    placed = (
        P("wide", "narrow"),
        P(),
        P(),
        P("wide", None),
        P("narrow", "wide"),
        P("narrow", "wide"),
        P("narrow", "wide"),
        P("wide", "narrow"),
        P(),
        P(),
    )
    return jax.shard_map(
        functools.partial(on_device, mesh.shape["wide"], mesh.shape["narrow"]),
        mesh=mesh,
        in_specs=placed,
        out_specs=P("wide", "narrow"),
        check_vma=False,
    )
```

time: 517 us -> 319 us (0.62)
  matrix products: 135 us -> 4.52 us
  waiting for transfers between devices: 252 us -> 146 us
  blocking collectives: 0 us -> 95.7 us
  local copies, waits for them, and re-layouts: 57.6 us -> 5.11 us
  other arithmetic: 54.1 us -> 5.93 us
  Pallas kernels: 0 us -> 41.5 us
  starting transfers between devices: 0.23 us -> 5.63 us
    dot_general x38 -> x1, matrix products: 135 us -> 4.52 us  [on_device(): lax.dot_general(normed, kv_rows, NT, preferred_element_type=F32)]
    all_gather x5 -> x6, waiting for transfers between devices: 176 us -> 68.6 us  [the longest x1 38.7 us: on_device(): lax.all_gather(attended, 'wide', axis=0)]
    all_to_all x0 -> x3, blocking collectives: none -> 85.4 us  [the longest x2 60.1 us: spread(): lax.all_to_all(weight, 'wide', split_axis=0, concat_axis=1, tiled=True)]
    reduce_sum x22 -> x1, other arithmetic: 46.6 us -> 1.51 us  [on_device(): jnp.mean(floats * floats, axis=1, keepdims=True) + EPS]
    pallas_call x0 -> x2, Pallas kernels: none -> 41.5 us  [the longest x1 27.5 us: on_device(): pl.pallas_call(functools.partial(attend_kernel, group), grid=(strands,),...]
    dynamic_slice x40 -> x1, local copies, waits for them, and re-layouts: 25.3 us -> 0.91 us  [on_device(): lax.dynamic_slice_in_dim(routes_all.reshape(strands, group, block, 2), su...]
    another operation x1 -> x0, local copies, waits for them, and re-layouts: 21.1 us -> none  [over_blocks(): cache_rows.reshape((steps_count, block_size) + cache_rows.shape[1:])]
    ppermute x0 -> x2, waiting for transfers between devices: none -> 16.7 us  [on_device(): pieces.append(lax.ppermute(chosen, ('wide', 'narrow'), pairs))]
  transfers between devices with their start and end apart: 7 -> 10, of which waited for: 5 -> 8; matrix products, arithmetic and copies ran while one was open for 45% -> 4% of each run, Pallas kernels for 0% -> 0%
where the time goes in v1:
time: 319 us; the launch traced here: 318 us
  waiting for transfers between devices  146 us (46%)
  blocking collectives  95.7 us (30%)
  Pallas kernels  41.5 us (13%)
  between operations  13.6 us (4%)
  other arithmetic  5.93 us (2%)
  starting transfers between devices  5.63 us (2%)
  local copies, waits for them, and re-layouts  5.11 us (2%)
  matrix products  4.52 us (1%)
    all_to_all x2, blocking collectives, spread(): lax.all_to_all(weight, 'wide', split_axis=0, concat_axis=1, tiled=True)  60.1 us
    reduce_scatter x1, waiting for transfers between devices, on_device(): lax.psum_scatter(partial_out, 'narrow', scatter_dimension=0, tiled=True)  43.4 us
    all_gather x1, waiting for transfers between devices, on_device(): lax.all_gather(attended, 'wide', axis=0)  38.7 us
    pallas_call x1, Pallas kernels, on_device(): pl.pallas_call(functools.partial(attend_kernel, group), grid=(strands,),...  27.5 us
    all_to_all x1, blocking collectives, on_device(): lax.all_to_all(prefix_cache, 'wide', split_axis=1, concat_axis=0, tiled=T...  25.3 us
    all_gather x1, waiting for transfers between devices, on_device(): whole = lax.all_gather(tokens, 'narrow', axis=1, tiled=True)  16.9 us
    ppermute x2, waiting for transfers between devices, on_device(): pieces.append(lax.ppermute(chosen, ('wide', 'narrow'), pairs))  16.7 us
    pallas_call x1, Pallas kernels, on_device(): pl.pallas_call(out_kernel, grid=(wide,), out_shape=jax.ShapeDtypeStruct((...  13.9 us
  transfers between devices with their start and end apart: 10, of which 8 were waited for; matrix products, arithmetic and copies ran while one was open for 4% of the time, Pallas kernels for 0%

profile of v1, /device:TPU:3, one launch (start us, length us, event | category | flops | bytes accessed | tf_op | source)
XLA Modules:
  0.0 318.5 jit_solution(3351483863994538118)
XLA Ops:
  6.5 0.0 copy-start
  6.5 0.0 all-gather.9.cloned.1.call-start
  6.5 0.7 all-gather.9.cloned.1.call-update
  7.3 0.0 all-gather.17.cloned.1.call-start
  7.3 12.6 %all_to_all.57 = bf16[8,128,256]{2,1,0:T(8,128)(2,1)S(1)} all-to-all(bf16[8,128,256]{2,1,0:T(8,128)(2,1)} %bitcast.42), channel_id=1, replica_groups=mesh['wide'=8,'narrow'=4] {'wide'}, dimensions={0} | all-to-all | bytes 1048576 | tf_op jit(solution)/shard_map/all_to_all | solution.py:183
  19.9 1.0 copy.27
  21.0 0.0 all-gather.17.cloned.1.call-update
  21.0 0.0 all-gather.11.cloned.1.call-start
  21.1 16.9 %all-gather.9.cloned.1.call-done = bf16[256,2048]{1,0:T(8,128)(2,1)} async-done(((bf16[256,512]{1,0:T(8,128)(2,1)}), bf16[256,2048]{1,0:T(8,128)(2,1)}) %all-gather.9.cloned.1.call-update) | async-done | bytes 1048592 | tf_op jit(solution)/shard_map/all_gather | solution.py:169
  38.0 1.5 fusion
  39.5 2.5 fusion.2
  42.0 0.0 all-gather.11.cloned.1.call-update
  42.0 0.0 all-gather.15.cloned.1.call-start
  42.1 0.3 copy_bitcast_fusion
  42.4 25.3 %all_to_all.58 = bf16[768,8,128]{2,0,1:T(8,128)(2,1)} all-to-all(bf16[768,8,128]{2,0,1:T(8,128)(2,1)S(1)} %copy_bitcast_fusion), channel_id=1, replica_groups=mesh['wide'=8,'narrow'=4] {'wide'}, dimensions={1} | all-to-all | bytes 3145728 | tf_op jit(solution)/shard_map/all_to_all | solution.py:188
  67.7 0.0 all-gather.15.cloned.1.call-update
  67.7 0.0 all-gather.13.cloned.1.call-start
  67.7 47.5 %all_to_all.59 = bf16[8,512,256]{2,1,0:T(8,128)(2,1)S(1)} all-to-all(bf16[8,512,256]{2,1,0:T(8,128)(2,1)} %bitcast.38), channel_id=1, replica_groups=mesh['wide'=8,'narrow'=4] {'wide'}, dimensions={0} | all-to-all | bytes 4194304 | tf_op jit(solution)/shard_map/all_to_all | solution.py:183
  115.2 1.7 copy.30
  116.9 0.0 all-gather.13.cloned.1.call-update
  117.0 0.0 copy-start.2
  117.0 0.0 copy-start.4
  117.0 0.0 all-gather.19.cloned.1.call-start
  117.0 0.0 all-gather.17.cloned.1.call-done
  117.1 7.0 %all-gather.11.cloned.1.call-done.normed_ref = bf16[1024,2048]{1,0:T(8,128)(2,1)} async-done(((bf16[256,2048]{1,0:T(8,128)(2,1)}), bf16[1024,2048]{1,0:T(8,128)(2,1)}) %all-gather.11.cloned.1.call-update) | async-done | bytes 4194320 | tf_op jit(solution)/shard_map/all_gather | solution.py:176
  124.1 4.5 %convolution_convert_fusion = bf16[1024,256]{1,0:T(8,128)(2,1)} fusion(bf16[1024,2048]{1,0:T(8,128)(2,1)} %all-gather.11.cloned.1.call-done.normed_ref, bf16[256,2048]{0,1:T(8,128)(2,1)} %all-gather.17.cloned.1.call-done), kind=kOutput, calls=%fused_computation.6 | convolution fusion | flops 1074003968 | bytes 5767168 | tf_op jit(solution)/shard_map/dot_general | solution.py:191
  128.6 0.0 all-gather.19.cloned.1.call-update
  128.6 0.0 all-gather.21.cloned.1.call-start
  128.7 1.0 copy.28.router_ref
  129.7 0.1 copy.25
  129.8 10.3 %all_gather.30.routes_ref = s32[2048,2]{1,0:T(8,128)S(1)} all-gather(s32[256,2]{1,0:T(8,128)S(1)} %copy.25), channel_id=1, replica_groups=mesh['wide'=8,'narrow'=4] {'wide'}, dimensions={0}, use_global_device_ids=true | all-gather | bytes 18432 | tf_op jit(solution)/shard_map/all_gather | solution.py:177
  140.1 0.9 constant_dynamic-slice_fusion
  141.1 11.3 %all-gather.13.cloned.1.call-done.query_ref = bf16[1024,2048]{1,0:T(8,128)(2,1)} async-done(((bf16[512,2048]{1,0:T(8,128)(2,1)}), bf16[1024,2048]{1,0:T(8,128)(2,1)}) %all-gather.13.cloned.1.call-update) | async-done | bytes 4194320 | tf_op jit(solution)/shard_map/all_gather | solution.py:184
  152.3 11.6 %all-gather.19.cloned.1.call-done.kv_ref = bf16[2048,256]{1,0:T(8,128)(2,1)} async-done(((bf16[1024,256]{1,0:T(8,128)(2,1)}), bf16[2048,256]{1,0:T(8,128)(2,1)}) %all-gather.19.cloned.1.call-update) | async-done | bytes 1048592 | tf_op jit(solution)/shard_map/all_gather | solution.py:192
  164.0 27.5 %attend.1 = bf16[2,1024,128]{2,1,0:T(8,128)(2,1)} custom-call(s32[4]{0:T(128)} %suffix_ref.1, s32[4]{0:T(128)} %prefix_ref.1, s32[1]{0:T(128)} %bitcast.sub_ref, bf16[1024,2048]{1,0:T(8,128)(2,1)} %all-gather.11.cloned.1.call-done.normed_ref, bf16[2048,8]{1,0:T(8,128)(2,1)} %copy.28.router_ref, bf16[1024,2048]{1,0:T(8,128)(2,1)} %all-gather.13.cloned.1.call-done.query_ref, ...), custom_call_target="tpu_custom_call" | custom-call | tf_op jit(solution)/shard_map/attend/pallas_call | solution.py:196
  191.5 0.0 all-gather.21.cloned.1.call-update
  191.5 0.0 reduce-scatter.2.cloned.1.call-start
  191.6 38.7 %all-gather.21.cloned.1.call-done = bf16[16,1024,128]{2,1,0:T(8,128)(2,1)} async-done(((bf16[2,1024,128]{2,1,0:T(8,128)(2,1)}), bf16[16,1024,128]{2,1,0:T(8,128)(2,1)}) %all-gather.21.cloned.1.call-update) | async-done | bytes 4194320 | tf_op jit(solution)/shard_map/all_gather | solution.py:217
  230.3 13.9 %project_out.1 = f32[2048,256]{1,0:T(8,128)} custom-call(bf16[4,2,2,1024,128]{4,3,2,1,0:T(8,128)(2,1)} %bitcast.36, bf16[4096,256]{1,0:T(8,128)(2,1)} %weight_ref.1, s32[2048,2]{1,0:T(8,128)} %copy-done.1), custom_call_target="tpu_custom_call" | custom-call | tf_op jit(solution)/shard_map/project_out/pallas_call | solution.py:220
  244.2 0.0 reduce-scatter.2.cloned.1.call-update
  244.2 43.4 %reduce-scatter.2.cloned.1.call-done = f32[512,256]{1,0:T(8,128)} async-done(((f32[2048,256]{1,0:T(8,128)}), f32[512,256]{1,0:T(8,128)}) %reduce-scatter.2.cloned.1.call-update) | async-done | bytes 524304 | tf_op jit(solution)/shard_map/reduce_scatter | solution.py:235
  287.6 1.1 convert_element_type.19
  288.8 1.9 collective-permute-start
  290.7 3.4 %collective-permute-start.1 = (bf16[256,256]{1,0:T(8,128)(2,1)S(1)}, bf16[256,256]{1,0:T(8,128)(2,1)S(1)}, u32[]{:S(2)}, u32[]{:S(2)}) collective-permute-start(bf16[256,256]{1,0:T(8,128)(2,1)S(1)} %get-tuple-element.7), channel_id=1, source_target_pairs={{0,4},{1,12},{2,20},{3,28},{4,0},{5,8},{6,16},{7,24},{8,5},{9,13},... | collective-permute-start | bytes 393224 | tf_op jit(solution)/shard_map/ppermute | solution.py:248
  294.1 13.2 %collective-permute-done = bf16[256,256]{1,0:T(8,128)(2,1)S(1)} collective-permute-done((bf16[256,256]{1,0:T(8,128)(2,1)S(1)}, bf16[256,256]{1,0:T(8,128)(2,1)S(1)}, u32[]{:S(2)}, u32[]{:S(2)}) %collective-permute-start) | collective-permute-done | bytes 131104 | tf_op jit(solution)/shard_map/ppermute | solution.py:248
  307.3 3.6 %collective-permute-done.1 = bf16[256,256]{1,0:T(8,128)(2,1)S(1)} collective-permute-done((bf16[256,256]{1,0:T(8,128)(2,1)S(1)}, bf16[256,256]{1,0:T(8,128)(2,1)S(1)}, u32[]{:S(2)}, u32[]{:S(2)}) %collective-permute-start.1) | collective-permute-done | bytes 131104 | tf_op jit(solution)/shard_map/ppermute | solution.py:248
  310.8 0.1 fusion.6
  310.9 0.7 pad_maximum_fusion
  (11 shorter events, 0.1 us)
Async XLA Ops:
  6.5 35.6 %copy-start = (bf16[768,1024]{1,0:T(8,128)(2,1)S(1)}, bf16[768,1024]{1,0:T(8,128)(2,1)}, u32[]{:S(2)}) copy-start(bf16[768,1024]{1,0:T(8,128)(2,1)} %param.17) | copy-start | bytes 4718596
  6.5 14.5 %copy-start.3 = (bf16[2048]{0:T(1024)(128)(2,1)S(1)}, bf16[2048]{0:T(1024)(128)(2,1)}, u32[]{:S(2)}) copy-start(bf16[2048]{0:T(1024)(128)(2,1)} %param.11) | copy-start | bytes 12292
  6.5 31.4 %all-gather.9.cloned.1.call-start = ((), (), s32[]{:S(2)}) async-start(), calls=%async_computation.4 | async-start | bytes 1310720 | tf_op jit(solution)/shard_map/all_gather | solution.py:169
  7.3 109.8 %all-gather.17.cloned.1.call-start = ((), (), s32[]{:S(2)}) async-start(), calls=%async_computation.8 | async-start | bytes 1572864 | tf_op jit(solution)/shard_map/all_gather | solution.py:184
  21.0 103.1 %all-gather.11.cloned.1.call-start = ((), (), s32[]{:S(2)}) async-start(), calls=%async_computation.5 | async-start | bytes 5242880 | tf_op jit(solution)/shard_map/all_gather | solution.py:176
  42.0 99.0 %all-gather.15.cloned.1.call-start = ((), (), s32[]{:S(2)}) async-start(), calls=%async_computation.7 | async-start | bytes 4718592 | tf_op jit(solution)/shard_map/all_gather | solution.py:189
  67.7 84.6 %all-gather.13.cloned.1.call-start = ((), (), s32[]{:S(2)}) async-start(), calls=%async_computation.6 | async-start | bytes 6291456 | tf_op jit(solution)/shard_map/all_gather | solution.py:184
  117.0 11.7 %copy-start.2 = (bf16[2048,8]{0,1:T(8,128)(2,1)S(1)}, bf16[2048,8]{0,1:T(8,128)(2,1)}, u32[]{:S(2)}) copy-start(bf16[2048,8]{0,1:T(8,128)(2,1)} %param.12) | copy-start | bytes 98308
  117.0 12.7 %copy-start.4 = (s32[256,2]{0,1:T(2,128)S(1)}, s32[256,2]{0,1:T(2,128)}, u32[]{:S(2)}) copy-start(s32[256,2]{0,1:T(2,128)} %param.13) | copy-start | bytes 6148
  117.0 47.0 %all-gather.19.cloned.1.call-start = ((), (), s32[]{:S(2)}) async-start(), calls=%async_computation.9 | async-start | bytes 1572864 | tf_op jit(solution)/shard_map/all_gather | solution.py:192
  128.6 101.7 %all-gather.21.cloned.1.call-start = ((), (), s32[]{:S(2)}) async-start(), calls=%async_computation.11 | async-start | bytes 4718592 | tf_op jit(solution)/shard_map/all_gather | solution.py:217
  140.1 51.4 %copy-start.1 = (s32[2048,2]{1,0:T(8,128)}, s32[2048,2]{1,0:T(8,128)S(1)}, u32[]{:S(2)}) copy-start(s32[2048,2]{1,0:T(8,128)S(1)} %all_gather.30.routes_ref) | copy-start | bytes 49156
  191.5 96.1 %reduce-scatter.2.cloned.1.call-start = ((), (), s32[]{:S(2)}) async-start(), calls=%async_computation.10 | async-start | bytes 2621440 | tf_op jit(solution)/shard_map/reduce_scatter | solution.py:235
  288.8 18.5 %collective-permute-start = (bf16[256,256]{1,0:T(8,128)(2,1)S(1)}, bf16[256,256]{1,0:T(8,128)(2,1)S(1)}, u32[]{:S(2)}, u32[]{:S(2)}) collective-permute-start(bf16[256,256]{1,0:T(8,128)(2,1)S(1)} %get-tuple-element.8), channel_id=1, source_target_pairs={{0,0},{1,8},{2,16},{3,24},{4,4},{5,12},{6,20},{7,28},{8,1},{9,9},{... | collective-permute-start | bytes 393224 | tf_op jit(solution)/shard_map/ppermute | solution.py:248
  290.7 20.1 %collective-permute-start.1 = (bf16[256,256]{1,0:T(8,128)(2,1)S(1)}, bf16[256,256]{1,0:T(8,128)(2,1)S(1)}, u32[]{:S(2)}, u32[]{:S(2)}) collective-permute-start(bf16[256,256]{1,0:T(8,128)(2,1)S(1)} %get-tuple-element.7), channel_id=1, source_target_pairs={{0,4},{1,12},{2,20},{3,28},{4,0},{5,8},{6,16},{7,24},{8,5},{9,13},... | collective-permute-start | bytes 393224 | tf_op jit(solution)/shard_map/ppermute | solution.py:248
Sparse Core Ops, SparseCore 0:
  8.9 29.0 all-gather.8
  39.5 9.6 all-gather.16
  51.0 72.9 all-gather.10
  125.4 10.4 all-gather.14
  137.4 14.9 all-gather.12
  153.7 10.1 all-gather.18
  191.7 38.5 all-gather.20
  244.3 43.2 reduce-scatter.1

commit v2 on v1

--- a/solution.py
+++ b/solution.py
@@ -23,6 +23,11 @@
     for expert, block in enumerate(blocks):
         found = jnp.where(routes_column == expert, block, found)
     return found
+
+
+def route_columns(routes_rows):
+    turned = jnp.transpose(routes_rows)
+    return turned[:, 0:1], turned[:, 1:2]
 
 
 def attend_kernel(
@@ -41,7 +46,7 @@
     normed = normed_ref[...]
     logits = jnp.dot(normed, router_ref[...], preferred_element_type=F32)
     expert_at = lax.broadcasted_iota(jnp.int32, logits.shape, 1)
-    route_a, route_b = routes_ref[:, 0:1], routes_ref[:, 1:2]
+    route_a, route_b = route_columns(routes_ref[token_block])
     logit_a = jnp.sum(jnp.where(expert_at == route_a, logits, 0.0), axis=1, keepdims=True)
     logit_b = jnp.sum(jnp.where(expert_at == route_b, logits, 0.0), axis=1, keepdims=True)
     top = jnp.maximum(logit_a, logit_b)
@@ -117,28 +122,220 @@
     carried = lax.fori_loop(lax.div(start_block, block), token_block + 1, over_suffix, carried)
     unused, totals, summed = carried
     attended = jnp.transpose(summed / totals)
-    out_ref[0] = (attended[:block] * gate_a).astype(BF16)
-    out_ref[1] = (attended[block:] * gate_b).astype(BF16)
-
-
-def out_kernel(attended_ref, weight_ref, routes_ref, out_ref):
-    heads = attended_ref.shape[0]
-    route_a, route_b = routes_ref[:, 0:1], routes_ref[:, 1:2]
-    total = jnp.zeros(out_ref.shape, F32)
-    for head in range(heads):
-        first, second = attended_ref[head, 0, 0], attended_ref[head, 0, 1]
-        nothing = jnp.zeros_like(first)
-        padded = jnp.concatenate(
-            [
-                jnp.where(route_a == e, first, jnp.where(route_b == e, second, nothing))
-                for e in range(E)
-            ],
-            axis=1,
-        )
-        total = total + jnp.dot(
-            padded, weight_ref[head * E * H:(head + 1) * E * H, :], preferred_element_type=F32
-        )
-    out_ref[...] = total
+    out_ref[0, 0] = (attended[:block] * gate_a).astype(BF16)
+    out_ref[0, 1] = (attended[block:] * gate_b).astype(BF16)
+
+
+def remote(source, target, send_sem, recv_sem, place):
+    return pltpu.make_async_remote_copy(
+        src_ref=source,
+        dst_ref=target,
+        send_sem=send_sem,
+        recv_sem=recv_sem,
+        device_id=place,
+        device_id_type=pl.DeviceIdType.MESH,
+    )
+
+
+def greet(place):
+    pl.semaphore_signal(
+        pltpu.get_barrier_semaphore(),
+        inc=1,
+        device_id=place,
+        device_id_type=pl.DeviceIdType.MESH,
+    )
+
+
+def finish_kernel(
+    wide, narrow, group, attended_ref, weight_ref, routes_ref, out_ref,
+    gathered, parts, got, mine, final,
+    ring_send, ring_recv, pair_send, pair_recv, pass_send, pass_recv,
+    deep_send, deep_recv, turn_send, turn_recv
+):
+    heads = wide // group
+    ratio = wide // narrow
+    block = attended_ref.shape[2]
+    columns = weight_ref.shape[1]
+    me, depth = lax.axis_index("wide"), lax.axis_index("narrow")
+    head, sub = lax.div(me, group), lax.rem(me, group)
+    turned = lax.div(me, ratio)
+    lane = lax.rem(me, ratio)
+
+    for k in range(1, wide):
+        greet((lax.rem(me + k, wide), depth))
+    for k in range(1, narrow):
+        greet((me, lax.rem(depth + k, narrow)))
+    for u in range(ratio):
+        @pl.when(jnp.logical_or(ratio * depth + u != me, turned != depth))
+        def _():
+            greet((ratio * depth + u, turned))
+    own_turn = (turned == depth).astype(jnp.int32)
+    pl.semaphore_wait(pltpu.get_barrier_semaphore(), wide - 1 + narrow - 1 + ratio - own_turn)
+
+    strand_at = [lax.rem(depth + 1 + k, heads) for k in range(heads)]
+    sibling = [head * group + lax.rem(sub + ks, group) for ks in range(group)]
+
+    def ring(k, ka):
+        i = strand_at[k]
+        other = lax.rem(head + ka, heads) * group + sub
+        return remote(
+            attended_ref.at[i], gathered.at[head, sub, i],
+            ring_send.at[k, ka], ring_recv.at[k, ka], (other, depth)
+        )
+
+    def ring_in(k, ka):
+        i = strand_at[k]
+        source = lax.rem(head + heads - ka, heads)
+        return remote(
+            attended_ref.at[i], gathered.at[source, sub, i],
+            ring_send.at[k, ka], ring_recv.at[k, ka], (source * group + sub, depth)
+        )
+
+    def pair(k, ks):
+        i = strand_at[k]
+        return remote(
+            attended_ref.at[i], gathered.at[head, sub, i],
+            pair_send.at[k, ks], pair_recv.at[k, ks], (sibling[ks], depth)
+        )
+
+    def pair_in(k, ks):
+        i = strand_at[k]
+        return remote(
+            attended_ref.at[i], gathered.at[head, lax.rem(sub + group - ks, group), i],
+            pair_send.at[k, ks], pair_recv.at[k, ks], (sibling[ks], depth)
+        )
+
+    def hand(k, ka, ks):
+        i = strand_at[k]
+        held = gathered.at[lax.rem(head + heads - ka, heads), sub, i]
+        return remote(held, held, pass_send.at[k, ka, ks], pass_recv.at[k, ka, ks], (sibling[ks], depth))
+
+    def hand_in(k, ka, ks):
+        i = strand_at[k]
+        held = gathered.at[
+            lax.rem(head + heads - ka, heads), lax.rem(sub + group - ks, group), i
+        ]
+        return remote(held, held, pass_send.at[k, ka, ks], pass_recv.at[k, ka, ks], (sibling[ks], depth))
+
+    for k in range(heads):
+        for ka in range(1, heads):
+            ring(k, ka).start()
+        for ks in range(1, group):
+            pair(k, ks).start()
+    for k in range(heads):
+        gathered[head, sub, strand_at[k]] = attended_ref[strand_at[k]]
+
+    def stage(k):
+        for ka in range(1, heads):
+            ring_in(k, ka).wait_recv()
+            for ks in range(1, group):
+                hand(k, ka, ks).start()
+
+    def arrive(k):
+        for ks in range(1, group):
+            pair_in(k, ks).wait_recv()
+            for ka in range(1, heads):
+                hand_in(k, ka, ks).wait_recv()
+
+    def project(which):
+        route_a, route_b = route_columns(routes_ref[which])
+        total = jnp.zeros((block, columns), F32)
+        for h in range(heads):
+            first = gathered[h, lax.rem(which, group), lax.div(which, group), 0]
+            second = gathered[h, lax.rem(which, group), lax.div(which, group), 1]
+            nothing = jnp.zeros_like(first)
+            padded = jnp.concatenate(
+                [
+                    jnp.where(route_a == e, first, jnp.where(route_b == e, second, nothing))
+                    for e in range(E)
+                ],
+                axis=1,
+            )
+            total = total + jnp.dot(
+                padded, weight_ref[h * E * H:(h + 1) * E * H, :], preferred_element_type=F32
+            )
+        return total
+
+    def deep(k):
+        to = lax.rem(depth + 1 + k, narrow)
+        return remote(parts.at[k], got.at[k], deep_send.at[k], deep_recv.at[k], (me, to))
+
+    one_each = narrow == heads
+    if one_each:
+        stage(0)
+    else:
+        for k in range(heads):
+            stage(k)
+        for k in range(heads):
+            arrive(k)
+    owned = []
+    for k in range(narrow):
+        if one_each:
+            if k + 1 < heads:
+                stage(k + 1)
+            arrive(k)
+        quarter = lax.rem(depth + 1 + k, narrow)
+        for u in range(ratio):
+            total = project(quarter * ratio + u)
+            if k < narrow - 1:
+                parts[k, u] = total.astype(BF16)
+            else:
+                owned.append(total)
+        if k < narrow - 1:
+            deep(k).start()
+    for k in range(narrow - 1):
+        deep(k).wait_recv()
+    for u in range(ratio):
+        total = owned[u]
+        for k in range(narrow - 1):
+            total = total + got[k, u].astype(F32)
+        mine[u] = total.astype(BF16)
+
+    def turn(u):
+        return remote(
+            mine.at[u], final.at[lane], turn_send.at[u], turn_recv.at[lane],
+            (ratio * depth + u, turned)
+        )
+
+    def turn_in(u):
+        return remote(
+            mine.at[u], final.at[u], turn_send.at[u], turn_recv.at[u],
+            (ratio * depth + u, turned)
+        )
+
+    for u in range(ratio):
+        apart = jnp.logical_or(ratio * depth + u != me, turned != depth)
+
+        @pl.when(apart)
+        def _():
+            turn(u).start()
+
+        @pl.when(jnp.logical_not(apart))
+        def _():
+            final[lane] = mine[u]
+
+    for u in range(ratio):
+        apart = jnp.logical_or(ratio * depth + u != me, turned != depth)
+
+        @pl.when(apart)
+        def _():
+            turn_in(u).wait_recv()
+
+        out_ref[:, u * columns:(u + 1) * columns] = final[u]
+
+    for k in range(heads):
+        for ka in range(1, heads):
+            ring(k, ka).wait_send()
+            for ks in range(1, group):
+                hand(k, ka, ks).wait_send()
+        for ks in range(1, group):
+            pair(k, ks).wait_send()
+    for k in range(narrow - 1):
+        deep(k).wait_send()
+    for u in range(ratio):
+        @pl.when(jnp.logical_or(ratio * depth + u != me, turned != depth))
+        def _():
+            turn(u).wait_send()
 
 
 def on_device(
@@ -174,10 +371,9 @@
         * norm_gain.astype(F32)
     ).astype(BF16)
     normed = lax.all_gather(normed, "wide", axis_index_groups=same_sub, axis=0, tiled=True)
-    routes_all = lax.all_gather(routes, "wide", axis=0, tiled=True)
-    routes_here = lax.dynamic_slice_in_dim(
-        routes_all.reshape(strands, group, block, 2), sub, 1, axis=1
-    ).reshape(strands * block, 2)
+    routes_all = lax.all_gather(
+        jnp.pad(jnp.transpose(routes), ((0, 6), (0, 0))), "wide", axis=0
+    )
 
     def spread(weight):
         mine = lax.all_to_all(weight, "wide", split_axis=0, concat_axis=1, tiled=True)
@@ -196,7 +392,7 @@
     attended = pl.pallas_call(
         functools.partial(attend_kernel, group),
         grid=(strands,),
-        out_shape=jax.ShapeDtypeStruct((2, strands * block, H), BF16),
+        out_shape=jax.ShapeDtypeStruct((strands, 2, block, H), BF16),
         in_specs=[
             smem,
             smem,
@@ -204,54 +400,46 @@
             pl.BlockSpec((block, width), lambda i: (i, 0)),
             whole_block(router),
             whole_block(query_rows),
-            pl.BlockSpec((block, 2), lambda i: (i, 0)),
+            whole_block(routes_all),
             whole_block(cache),
             whole_block(kv),
         ],
-        out_specs=pl.BlockSpec((2, block, H), lambda i: (0, i, 0)),
+        out_specs=pl.BlockSpec((1, 2, block, H), lambda i: (i, 0, 0, 0)),
         compiler_params=pltpu.CompilerParams(vmem_limit_bytes=56 * 1024 * 1024),
         name="attend",
     )(
-        suffix_lengths, prefix_lengths, sub[None], normed, router, query_rows, routes_here, cache, kv
-    )
-    attended = lax.all_gather(attended, "wide", axis=0).reshape(
-        heads, group, 2, strands * block, H
-    )
-    partial_out = pl.pallas_call(
-        out_kernel,
-        grid=(wide,),
-        out_shape=jax.ShapeDtypeStruct((wide * block, columns), F32),
-        in_specs=[
-            pl.BlockSpec(
-                (heads, 1, 2, block, H), lambda i: (0, lax.rem(i, group), 0, lax.div(i, group), 0)
-            ),
-            whole_block(out_weight),
-            pl.BlockSpec((block, 2), lambda i: (i, 0)),
+        suffix_lengths, prefix_lengths, sub[None], normed, router, query_rows, routes_all, cache, kv
+    )
+    ratio = wide // narrow
+    in_vmem = pl.BlockSpec(memory_space=pltpu.VMEM)
+    dma = pltpu.SemaphoreType.DMA
+    return pl.pallas_call(
+        functools.partial(finish_kernel, wide, narrow, group),
+        out_shape=jax.ShapeDtypeStruct((block, ratio * columns), BF16),
+        in_specs=[in_vmem] * 3,
+        out_specs=in_vmem,
+        scratch_shapes=[
+            pltpu.VMEM((heads, group, strands, 2, block, H), BF16),
+            pltpu.VMEM((narrow - 1, ratio, block, columns), BF16),
+            pltpu.VMEM((narrow - 1, ratio, block, columns), BF16),
+            pltpu.VMEM((ratio, block, columns), BF16),
+            pltpu.VMEM((ratio, block, columns), BF16),
+            dma((heads, heads)),
+            dma((heads, heads)),
+            dma((heads, group)),
+            dma((heads, group)),
+            dma((heads, heads, group)),
+            dma((heads, heads, group)),
+            dma((narrow,)),
+            dma((narrow,)),
+            dma((ratio,)),
+            dma((ratio,)),
         ],
-        out_specs=pl.BlockSpec((block, columns), lambda i: (i, 0)),
-        compiler_params=pltpu.CompilerParams(vmem_limit_bytes=56 * 1024 * 1024),
-        name="project_out",
+        compiler_params=pltpu.CompilerParams(
+            vmem_limit_bytes=56 * 1024 * 1024, collective_id=1, has_side_effects=True
+        ),
+        name="finish",
     )(attended, out_weight, routes_all)
-    mine = lax.psum_scatter(partial_out, "narrow", scatter_dimension=0, tiled=True).astype(BF16)
-    ratio = wide // narrow
-    mine = mine.reshape(ratio, block, columns)
-    which = lax.rem(me, ratio)
-    pieces = []
-    for turn in range(ratio):
-        chosen = lax.dynamic_index_in_dim(mine, lax.rem(which + turn, ratio), 0, keepdims=False)
-        pairs = []
-        for w in range(wide):
-            for n in range(narrow):
-                to_wide = ratio * n + (w % ratio + turn) % ratio
-                to_narrow = w // ratio
-                pairs.append((w * narrow + n, to_wide * narrow + to_narrow))
-        pieces.append(lax.ppermute(chosen, ("wide", "narrow"), pairs))
-    stacked = jnp.stack(pieces)
-    ordered = [
-        lax.dynamic_index_in_dim(stacked, lax.rem(which - k + ratio, ratio), 0, keepdims=False)
-        for k in range(ratio)
-    ]
-    return jnp.concatenate(ordered, axis=1)
 
 
 def solution(mesh):

time: 319 us -> 270 us (0.85)
  waiting for transfers between devices: 146 us -> 49.2 us
  Pallas kernels: 41.5 us -> 98.7 us
  starting transfers between devices: 5.63 us -> 0.21 us
    pallas_call x1, Pallas kernels: 13.9 us -> 65.1 us  [on_device(): pl.pallas_call(functools.partial(finish_kernel, wide, narrow, group), out...]
    reduce_scatter x1 -> x0, waiting for transfers between devices: 43.4 us -> none  [on_device(): lax.psum_scatter(partial_out, 'narrow', scatter_dimension=0, tiled=True)]
    all_gather x1 -> x0, waiting for transfers between devices: 38.7 us -> none  [on_device(): lax.all_gather(attended, 'wide', axis=0)]
    ppermute x2 -> x0, waiting for transfers between devices: 16.7 us -> none  [on_device(): pieces.append(lax.ppermute(chosen, ('wide', 'narrow'), pairs))]
    pallas_call x1, Pallas kernels: 27.5 us -> 33.7 us  [on_device(): pl.pallas_call(functools.partial(attend_kernel, group), grid=(strands,),...]
    ppermute x2 -> x0, starting transfers between devices: 5.33 us -> none  [on_device(): pieces.append(lax.ppermute(chosen, ('wide', 'narrow'), pairs))]
  transfers between devices with their start and end apart: 10 -> 6, of which waited for: 8 -> 4; matrix products, arithmetic and copies ran while one was open for 4% -> 5% of each run, Pallas kernels for 0% -> 0%
where the time goes in v2:
time: 270 us; the launch traced here: 271 us
  Pallas kernels  98.7 us (37%)
  blocking collectives  94.9 us (35%)
  waiting for transfers between devices  49.2 us (18%)
  between operations  13.6 us (5%)
  local copies, waits for them, and re-layouts  5.73 us (2%)
  matrix products  4.54 us (2%)
  other arithmetic  4.04 us (1%)
    pallas_call x1, Pallas kernels, on_device(): pl.pallas_call(functools.partial(finish_kernel, wide, narrow, group), out...  65.1 us
    all_to_all x2, blocking collectives, spread(): lax.all_to_all(weight, 'wide', split_axis=0, concat_axis=1, tiled=True)  60.1 us
    pallas_call x1, Pallas kernels, on_device(): pl.pallas_call(functools.partial(attend_kernel, group), grid=(strands,),...  33.7 us
    all_to_all x1, blocking collectives, on_device(): lax.all_to_all(prefix_cache, 'wide', split_axis=1, concat_axis=0, tiled=T...  25.3 us
    all_gather x1, waiting for transfers between devices, on_device(): whole = lax.all_gather(tokens, 'narrow', axis=1, tiled=True)  16.9 us
    all_gather x2, waiting for transfers between devices, spread(): lax.all_gather(mine, 'wide', axis_index_groups=same_head, axis=0, tiled=T...  12.8 us
    all_gather x1, waiting for transfers between devices, on_device(): lax.all_gather(kv, 'wide', axis_index_groups=same_head, axis=0, tiled=True)  11.6 us
    all_gather x1, blocking collectives, on_device(): lax.all_gather(jnp.pad(jnp.transpose(routes), ((0, 6), (0, 0))), 'wide',...  9.5 us
  transfers between devices with their start and end apart: 6, of which 4 were waited for; matrix products, arithmetic and copies ran while one was open for 5% of the time, Pallas kernels for 0%

profile of v2, /device:TPU:3, one launch (start us, length us, event | category | flops | bytes accessed | tf_op | source)
XLA Modules:
  0.0 270.9 jit_solution(8221769459203615603)
XLA Ops:
  6.5 0.0 copy-start
  6.5 0.0 copy-start.2
  6.5 0.0 all-gather.8.cloned.1.call-start
  6.5 0.7 all-gather.8.cloned.1.call-update
  7.3 0.0 all-gather.16.cloned.1.call-start
  7.3 12.6 %all_to_all.57 = bf16[8,128,256]{2,1,0:T(8,128)(2,1)S(1)} all-to-all(bf16[8,128,256]{2,1,0:T(8,128)(2,1)} %bitcast.28), channel_id=1, replica_groups=mesh['wide'=8,'narrow'=4] {'wide'}, dimensions={0} | all-to-all | bytes 1048576 | tf_op jit(solution)/shard_map/all_to_all | solution.py:379
  19.9 1.0 copy.23
  20.9 0.0 all-gather.16.cloned.1.call-update
  21.0 0.0 all-gather.10.cloned.1.call-start
  21.0 0.0 copy-done.2
  21.0 16.9 %all-gather.8.cloned.1.call-done = bf16[256,2048]{1,0:T(8,128)(2,1)} async-done(((bf16[256,512]{1,0:T(8,128)(2,1)}), bf16[256,2048]{1,0:T(8,128)(2,1)}) %all-gather.8.cloned.1.call-update) | async-done | bytes 1048592 | tf_op jit(solution)/shard_map/all_gather | solution.py:366
  38.0 1.5 fusion
  39.5 2.5 fusion.2
  42.0 0.0 all-gather.10.cloned.1.call-update
  42.0 0.0 all-gather.14.cloned.1.call-start
  42.1 0.0 copy-done
  42.1 0.3 copy_bitcast_fusion
  42.4 25.3 %all_to_all.58 = bf16[768,8,128]{2,0,1:T(8,128)(2,1)} all-to-all(bf16[768,8,128]{2,0,1:T(8,128)(2,1)S(1)} %copy_bitcast_fusion), channel_id=1, replica_groups=mesh['wide'=8,'narrow'=4] {'wide'}, dimensions={1} | all-to-all | bytes 3145728 | tf_op jit(solution)/shard_map/all_to_all | solution.py:384
  67.7 0.0 all-gather.14.cloned.1.call-update
  67.7 0.0 all-gather.12.cloned.1.call-start
  67.7 47.5 %all_to_all.59 = bf16[8,512,256]{2,1,0:T(8,128)(2,1)S(1)} all-to-all(bf16[8,512,256]{2,1,0:T(8,128)(2,1)} %bitcast.23), channel_id=1, replica_groups=mesh['wide'=8,'narrow'=4] {'wide'}, dimensions={0} | all-to-all | bytes 4194304 | tf_op jit(solution)/shard_map/all_to_all | solution.py:379
  115.2 1.7 copy.26
  117.0 0.0 all-gather.12.cloned.1.call-update
  117.0 0.0 copy-start.1
  117.0 0.0 copy-start.3
  117.0 0.0 all-gather.18.cloned.1.call-start
  117.1 0.0 all-gather.16.cloned.1.call-done
  117.1 7.0 %all-gather.10.cloned.1.call-done.normed_ref = bf16[1024,2048]{1,0:T(8,128)(2,1)} async-done(((bf16[256,2048]{1,0:T(8,128)(2,1)}), bf16[1024,2048]{1,0:T(8,128)(2,1)}) %all-gather.10.cloned.1.call-update) | async-done | bytes 4194320 | tf_op jit(solution)/shard_map/all_gather | solution.py:373
  124.1 4.5 %convolution_convert_fusion = bf16[1024,256]{1,0:T(8,128)(2,1)} fusion(bf16[1024,2048]{1,0:T(8,128)(2,1)} %all-gather.10.cloned.1.call-done.normed_ref, bf16[256,2048]{0,1:T(8,128)(2,1)} %all-gather.16.cloned.1.call-done), kind=kOutput, calls=%fused_computation.6 | convolution fusion | flops 1074003968 | bytes 5767168 | tf_op jit(solution)/shard_map/dot_general | solution.py:387
  128.6 0.0 all-gather.18.cloned.1.call-update
  128.6 0.0 copy-done.1
  128.6 1.0 copy.24.router_ref
  129.7 0.0 copy-done.3
  129.7 9.5 %all-gather = s32[64,256]{1,0:T(8,128)} all-gather(s32[8,256]{1,0:T(8,128)S(1)} %pad.4), channel_id=2, replica_groups=mesh['wide'=8,'narrow'=4] {'wide'}, dimensions={0}, use_global_device_ids=true | all-gather | bytes 73728 | tf_op jit(solution)/shard_map/all_gather | solution.py:374
  139.2 0.0 all-gather.14.cloned.1.call-done.cache_ref
  139.2 12.8 %all-gather.12.cloned.1.call-done.query_ref = bf16[1024,2048]{1,0:T(8,128)(2,1)} async-done(((bf16[512,2048]{1,0:T(8,128)(2,1)}), bf16[1024,2048]{1,0:T(8,128)(2,1)}) %all-gather.12.cloned.1.call-update) | async-done | bytes 4194320 | tf_op jit(solution)/shard_map/all_gather | solution.py:380
  152.0 11.6 %all-gather.18.cloned.1.call-done.kv_ref = bf16[2048,256]{1,0:T(8,128)(2,1)} async-done(((bf16[1024,256]{1,0:T(8,128)(2,1)}), bf16[2048,256]{1,0:T(8,128)(2,1)}) %all-gather.18.cloned.1.call-update) | async-done | bytes 1048592 | tf_op jit(solution)/shard_map/all_gather | solution.py:388
  163.6 33.7 %attend.1.attended_ref = bf16[4,2,256,128]{3,2,1,0:T(8,128)(2,1)} custom-call(s32[4]{0:T(128)} %suffix_ref.1, s32[4]{0:T(128)} %prefix_ref.1, s32[1]{0:T(128)} %bitcast.sub_ref, bf16[1024,2048]{1,0:T(8,128)(2,1)} %all-gather.10.cloned.1.call-done.normed_ref, bf16[2048,8]{1,0:T(8,128)(2,1)} %copy.24.router_ref, ...), custom_call_target="tpu_custom_call" | custom-call | tf_op jit(solution)/shard_map/attend/pallas_call | solution.py:392
  197.3 65.1 %finish.1 = bf16[256,512]{1,0:T(8,128)(2,1)} custom-call(bf16[4,2,256,128]{3,2,1,0:T(8,128)(2,1)} %attend.1.attended_ref, bf16[4096,256]{1,0:T(8,128)(2,1)} %weight_ref.1, s32[8,8,256]{2,1,0:T(8,128)} %bitcast.27), custom_call_target="tpu_custom_call" | custom-call | tf_op jit(solution)/shard_map/finish/pallas_call | solution.py:416
  262.4 1.7 copy.29
  (3 shorter events, 0.0 us)
Async XLA Ops:
  6.5 35.6 %copy-start = (bf16[768,1024]{1,0:T(8,128)(2,1)S(1)}, bf16[768,1024]{1,0:T(8,128)(2,1)}, u32[]{:S(2)}) copy-start(bf16[768,1024]{1,0:T(8,128)(2,1)} %param.17) | copy-start | bytes 4718596
  6.5 14.5 %copy-start.2 = (bf16[2048]{0:T(1024)(128)(2,1)S(1)}, bf16[2048]{0:T(1024)(128)(2,1)}, u32[]{:S(2)}) copy-start(bf16[2048]{0:T(1024)(128)(2,1)} %param.11) | copy-start | bytes 12292
  6.5 31.4 %all-gather.8.cloned.1.call-start = ((), (), s32[]{:S(2)}) async-start(), calls=%async_computation.3 | async-start | bytes 1310720 | tf_op jit(solution)/shard_map/all_gather | solution.py:366
  7.3 109.8 %all-gather.16.cloned.1.call-start = ((), (), s32[]{:S(2)}) async-start(), calls=%async_computation.7 | async-start | bytes 1572864 | tf_op jit(solution)/shard_map/all_gather | solution.py:380
  21.0 103.1 %all-gather.10.cloned.1.call-start = ((), (), s32[]{:S(2)}) async-start(), calls=%async_computation.4 | async-start | bytes 5242880 | tf_op jit(solution)/shard_map/all_gather | solution.py:373
  42.0 97.1 %all-gather.14.cloned.1.call-start = ((), (), s32[]{:S(2)}) async-start(), calls=%async_computation.6 | async-start | bytes 4718592 | tf_op jit(solution)/shard_map/all_gather | solution.py:385
  67.7 84.3 %all-gather.12.cloned.1.call-start = ((), (), s32[]{:S(2)}) async-start(), calls=%async_computation.5 | async-start | bytes 6291456 | tf_op jit(solution)/shard_map/all_gather | solution.py:380
  117.0 11.7 %copy-start.1 = (bf16[2048,8]{0,1:T(8,128)(2,1)S(1)}, bf16[2048,8]{0,1:T(8,128)(2,1)}, u32[]{:S(2)}) copy-start(bf16[2048,8]{0,1:T(8,128)(2,1)} %param.12) | copy-start | bytes 98308
  117.0 12.7 %copy-start.3 = (s32[256,2]{0,1:T(2,128)S(1)}, s32[256,2]{0,1:T(2,128)}, u32[]{:S(2)}) copy-start(s32[256,2]{0,1:T(2,128)} %param.13) | copy-start | bytes 6148
  117.0 46.6 %all-gather.18.cloned.1.call-start = ((), (), s32[]{:S(2)}) async-start(), calls=%async_computation.8 | async-start | bytes 1572864 | tf_op jit(solution)/shard_map/all_gather | solution.py:388
Sparse Core Ops, SparseCore 0:
  8.9 29.0 all-gather.7
  39.5 9.6 all-gather.15
  51.0 72.9 all-gather.9
  125.4 10.2 all-gather.13
  137.1 14.8 all-gather.11
  153.4 10.1 all-gather.17
